TPU v7x, 128 devices: a whole 4x4x4 slice. The times are simulated.
128 devices in a mesh: row: 16 (over x, y), col: 8 (over z, core).
Axes of the slice: x: 4, y: 4, z: 4, core: 2. Of those that a mesh axis runs over, the one named last changes fastest.
Arguments:
- residual: bfloat16 [1024, 16, 5120], P('row', None, 'col'), may hold values from -6 to 6
- positions: int32 [1024], P('row'), may hold values from 0 to 15
- norm_gain: float32 [5120], P('col'), may hold values from 0.1 to 1.9
- w_gate: bfloat16 [5120, 16384], P('col', 'row'), may hold values from -0.078125 to 0.078125
- w_up: bfloat16 [5120, 16384], P('col', 'row'), may hold values from -0.078125 to 0.078125
- covariance: float32 [16384, 16384], P('row', 'col'), may hold values from -1 to 4, as said below
Outputs:
- factor: float32 [16384, 16384], P('row', 'col')
Inputs may be any that keep to these rules, and one draw needn't show every extreme that they name: `covariance`: symmetric positive definite in the natural order of hidden units.
All inputs are finite; a program needn't handle non-finite values.
Results may differ from a plain program's by a relative error of at most 0.0041.
Values may be sent and summed in bfloat16 or wider, within the bound.
A program may use at most 128 MiB of HBM per device.

v0:
```python
import functools
import jax
import jax.numpy as jnp
from jax import lax
from jax.sharding import Mesh
from jax.sharding import PartitionSpec as P

TILE = 64
PANEL = 256
NPANEL = 2
ROW = ("row_0", "row_1")
EPSILON = 1e-06
HIGHEST_PRECISION = lax.Precision.HIGHEST


def by_axis(array, axes):
    return functools.reduce(lax.psum, axes, array)


def copy_for_each(array, axis):
    copies = jnp.broadcast_to(array, (lax.axis_size(axis), *array.shape))
    return lax.all_to_all(copies, axis, split_axis=0, concat_axis=0, tiled=True)


def of_everyone(array, axis):
    everything = copy_for_each(array, axis)
    return jnp.sum(everything, axis=0)


def joined_along(pieces, dim):
    lengths = list(pieces.shape[1:])
    lengths[dim] *= pieces.shape[0]
    return jnp.moveaxis(pieces, 0, dim).reshape(lengths)


def gathered_copies(array, axis, dim):
    return joined_along(copy_for_each(array, axis), dim)


def shortened(array):

    def short(part):
        return part.astype(jnp.bfloat16) if part.dtype == jnp.float32 else part

    return jax.tree.map(short, array)


def broadcast(value, axis, source):
    kept = jnp.where(lax.axis_index(axis) == source, value, 0).astype(value.dtype)
    return lax.psum(kept, axis)


def trailing(left_factor, right_factor):
    return lax.dot_general(
        left_factor,
        right_factor,
        (((1,), (1,)), ((), ())),
        precision=HIGHEST_PRECISION,
        preferred_element_type=jnp.float32,
    )


def unit_scale(raw_keys, wide_hidden):
    squares = by_axis(jnp.sum(raw_keys * raw_keys, axis=1), ROW)
    return (raw_keys * lax.rsqrt(squares / wide_hidden + EPSILON)[:, None]).astype(jnp.bfloat16)


def on_device(residual, positions, norm_gain, w_gate, w_up, covariance):
    row_devices = lax.axis_size(ROW)
    col_devices = lax.axis_size("col")
    row_rank = lax.axis_index(ROW)
    col_rank = lax.axis_index("col")
    local_prompts = residual.shape[0]
    token_count = residual.shape[1]
    local_feat = residual.shape[2]
    model_width = local_feat * col_devices
    hidden_local = w_gate.shape[1]
    wide_hidden = hidden_local * row_devices
    row_count = covariance.shape[0]
    col_count = covariance.shape[1]
    tiles_here = hidden_local // TILE
    panel_tiles = PANEL // TILE
    token_iota = lax.broadcasted_iota(jnp.int32, (local_prompts, token_count), 1)
    token_mask = (token_iota == positions[:, None])[:, :, None]
    picked = jnp.where(token_mask, residual, jnp.zeros_like(residual))
    subject = jnp.sum(picked.astype(jnp.float32), axis=1)
    part_squares = jnp.sum(subject * subject, axis=1)
    total_squares = of_everyone(part_squares, "col")
    inverse_rms = lax.rsqrt(total_squares / model_width + EPSILON)
    normed = (subject * inverse_rms[:, None] * norm_gain[None, :]).astype(jnp.bfloat16)
    normed_all = gathered_copies(normed, ROW, 0)
    prompts = normed_all.shape[0]
    gate_block = jnp.dot(normed_all, w_gate, preferred_element_type=jnp.float32)
    up_block = jnp.dot(normed_all, w_up, preferred_element_type=jnp.float32)
    shared = lax.psum_scatter(
        jnp.concatenate([gate_block, up_block], axis=1), "col", scatter_dimension=0, tiled=True
    )
    unit_share = unit_scale(
        jax.nn.silu(shared[:, :hidden_local]) * shared[:, hidden_local:], wide_hidden
    )
    unit_keys = gathered_copies(unit_share, "col", 0)
    grouped = (
        unit_keys.reshape(prompts, tiles_here // row_devices, row_devices, TILE)
        .transpose(0, 2, 1, 3)
        .reshape(prompts, hidden_local)
    )
    row_keys = lax.all_to_all(grouped, ROW, split_axis=1, concat_axis=1, tiled=True)
    col_split = unit_keys.reshape(prompts, tiles_here // col_devices, col_devices, TILE)
    col_pick = lax.dynamic_index_in_dim(col_split, col_rank, axis=2, keepdims=False).reshape(
        prompts, tiles_here // col_devices * TILE
    )
    col_keys = lax.all_gather(col_pick, ROW, axis=1, tiled=True)
    keys_outer = lax.dot_general(
        row_keys, col_keys, (((0,), (0,)), ((), ())), preferred_element_type=jnp.float32
    )
    updated = covariance + keys_outer * (1.0 / prompts)
    row_pos = lax.broadcasted_iota(jnp.int32, (row_count,), 0)
    row_global = (row_pos // TILE * row_devices + row_rank) * TILE + row_pos % TILE
    col_pos = lax.broadcasted_iota(jnp.int32, (col_count,), 0)
    col_global = (col_pos // TILE * col_devices + col_rank) * TILE + col_pos % TILE
    row_groups = row_devices // col_devices
    panel_iota = lax.broadcasted_iota(jnp.int32, (1, PANEL), 1)

    def col_bounds(number):
        first_tile = number * panel_tiles
        col_start = first_tile // col_devices
        col_end = (first_tile + panel_tiles - 1) // col_devices + 1
        return (col_start * TILE, col_end * TILE)

    for number in range(NPANEL):
        begin_col, end_col = col_bounds(number)
        factor_first_tile = number * panel_tiles
        factor_col_start = factor_first_tile // col_devices
        col_tiles = (factor_first_tile + panel_tiles - 1) // col_devices + 1 - factor_col_start
        gathered = gathered_copies(updated[:, begin_col:end_col], "col", 1)
        gathered = (
            gathered.reshape(row_count, col_devices, col_tiles, TILE)
            .transpose(0, 2, 1, 3)
            .reshape(row_count, col_tiles * col_devices * TILE)
        )
        col_offset = (factor_first_tile - factor_col_start * col_devices) * TILE
        panel_rows = gathered[:, col_offset : col_offset + PANEL]
        row_start = factor_first_tile // row_devices
        row_tiles = (factor_first_tile + panel_tiles - 1) // row_devices + 1 - row_start
        diag_rows = gathered_copies(
            panel_rows[row_start * TILE : (row_start + row_tiles) * TILE].astype(jnp.bfloat16),
            ROW,
            0,
        ).astype(jnp.float32)
        diag_rows = (
            diag_rows.reshape(row_devices, row_tiles, TILE, PANEL)
            .transpose(1, 0, 2, 3)
            .reshape(row_tiles * row_devices * TILE, PANEL)
        )
        row_offset = (factor_first_tile - row_start * row_devices) * TILE
        lower_factor = jnp.linalg.cholesky(diag_rows[row_offset : row_offset + PANEL])
        solved = jax.scipy.linalg.solve_triangular(lower_factor, panel_rows.T, lower=True).T
        factor_shifted = row_global - number * PANEL
        selector = (factor_shifted[:, None] == panel_iota).astype(jnp.float32)
        from_lower = jnp.dot(
            selector, lower_factor, precision=HIGHEST_PRECISION, preferred_element_type=jnp.float32
        )
        factor_panel_factor = jnp.where((factor_shifted >= PANEL)[:, None], solved, from_lower)
        received = []
        for member in range(row_groups):
            received.append(
                broadcast(
                    shortened(factor_panel_factor), ROW, col_rank + member * col_devices
                ).astype(factor_panel_factor.dtype)
            )
        column_factor = (
            jnp.stack(received, 0)
            .reshape(row_groups, row_count // TILE, TILE, PANEL)
            .transpose(1, 0, 2, 3)
            .reshape(col_count, PANEL)
        )
        panel_factor, column_factor = (factor_panel_factor, column_factor)
        updated = updated - trailing(panel_factor, column_factor)
        place_begin_col, place_end_col = col_bounds(number)
        shifted = col_global[place_begin_col:place_end_col] - number * PANEL
        within = (shifted >= 0) & (shifted < PANEL)
        column_select = (panel_iota[0][:, None] == shifted[None, :]).astype(jnp.float32)
        values = jnp.dot(
            panel_factor,
            column_select,
            precision=HIGHEST_PRECISION,
            preferred_element_type=jnp.float32,
        )
        replaced = jnp.where(within[None, :], values, updated[:, place_begin_col:place_end_col])
        updated = updated.at[:, place_begin_col:place_end_col].set(replaced)
    lower_part = row_global[:, None] >= col_global[None, :]
    return jnp.where(lower_part, updated, 0.0)


def solution(mesh):
    torus = Mesh(mesh.devices.reshape(4, 4, mesh.shape["col"]), ("row_0", "row_1", "col"))
    placed = (P(ROW, None, "col"), P(ROW), P("col"), P("col", ROW), P("col", ROW), P(ROW, "col"))
    return jax.shard_map(
        on_device, mesh=torus, in_specs=placed, out_specs=P(ROW, "col"), check_vma=False
    )
```

profile of v0, /device:TPU:0, one launch (start us, length us, event | category | flops | bytes accessed | tf_op | source)
XLA Modules:
  0.0 690.5 jit_solution(8219200208824315445)
XLA Ops:
  7.4 2.0 convert_reduce_fusion
  10.1 5.4 all-to-all-start
  15.6 5.1 all-to-all-done
  21.7 26.6 %all_to_all.48 = bf16[16,64,640]{2,1,0:T(8,128)(2,1)S(1)} all-to-all(bf16[16,64,640]{2,1,0:T(8,128)(2,1)S(1)} %broadcast_in_dim.88), channel_id=1, replica_groups=mesh['row_0'=4,'row_1'=4,'col'=8] {'row_0','row_1'}, dimensions={0} | all-to-all | bytes 2621440 | tf_op jit(solution)/shard_map/all_to_all | solution.py:22
  48.2 1.9 fusion.61
  50.1 1.9 fusion.60
  52.0 4.2 pad_maximum_fusion
  56.2 49.1 %reduce-scatter.2.cloned.1.call-done = f32[128,2048]{0,1:T(8,128)} async-done(((f32[1024,2048]{0,1:T(8,128)}), f32[128,2048]{0,1:T(8,128)}) %reduce-scatter.2.cloned.1.call-update) | async-done | bytes 1048592 | tf_op jit(solution)/shard_map/reduce_scatter | solution.py:95
  105.3 1.4 multiply_reduce_fusion
  106.7 10.4 %psum.42 = f32[128]{0:T(128)S(1)} all-reduce(f32[128]{0:T(128)S(1)} %get-tuple-element.67), channel_id=1, replica_groups=mesh['row_0'=4,'row_1'=4,'col'=8] {'row_0'}, use_global_device_ids=true, to_apply=%region_5.6 | all-reduce | flops 128 | bytes 1024 | tf_op jit(solution)/shard_map/psum | solution.py:17
  117.1 10.5 %psum.43 = f32[128]{0:T(128)S(1)} all-reduce(f32[128]{0:T(128)S(1)} %psum.42), channel_id=1, replica_groups=mesh['row_0'=4,'row_1'=4,'col'=8] {'row_1'}, use_global_device_ids=true, to_apply=%region_6.7 | all-reduce | flops 128 | bytes 1024 | tf_op jit(solution)/shard_map/psum | solution.py:17
  127.6 1.6 broadcast_in_dim.89
  129.2 4.3 all-to-all-start.2
  133.6 27.1 %all-to-all-done.2 = bf16[8,128,1024]{1,2,0:T(8,128)(2,1)} async-done(((bf16[8,128,1024]{1,2,0:T(8,128)(2,1)}), bf16[8,128,1024]{1,2,0:T(8,128)(2,1)}, u32[]{:S(2)}, u32[]{:S(2)}) %all-to-all-start.2) | async-done | bytes 2097184 | tf_op jit(solution)/shard_map/all_to_all | solution.py:22
  160.8 2.9 copy.81
  163.7 2.3 reshape_reshape.3
  166.0 1.7 constant_dynamic-slice_fusion.2
  167.7 2.3 all_to_all.33
  170.0 35.8 %all_to_all.49 = bf16[1024,16,64]{0,2,1:T(8,128)(2,1)S(1)} all-to-all(bf16[1024,16,64]{0,2,1:T(8,128)(2,1)} %all_to_all.33), channel_id=1, replica_groups=mesh['row_0'=4,'row_1'=4,'col'=8] {'row_0','row_1'}, dimensions={1} | all-to-all | bytes 4194304 | tf_op jit(solution)/shard_map/all_to_all | solution.py:107
  205.8 24.1 %all-gather.2.cloned.1.call-done = bf16[1024,2048]{0,1:T(8,128)(2,1)} async-done(((bf16[1024,128]{0,1:T(8,128)(2,1)}), bf16[1024,2048]{0,1:T(8,128)(2,1)}) %all-gather.2.cloned.1.call-update) | async-done | bytes 4194320 | tf_op jit(solution)/shard_map/all_gather | solution.py:112
  229.9 8.2 %multiply_add_fusion = f32[1024,2048]{1,0:T(8,128)S(1)} fusion(f32[1024,2048]{1,0:T(8,128)} %param.18, bf16[1024,1024]{0,1:T(8,128)(2,1)S(1)} %bitcast.126, bf16[1024,2048]{0,1:T(8,128)(2,1)} %all-gather.2.cloned.1.call-done), kind=kOutput, calls=%fused_computation.5 | convolution fusion | flops 4299161600 | bytes 23068672 | tf_op jit(solution)/shard_map/dot_general | solution.py:113
  238.1 3.4 copy-done.4
  241.8 1.6 broadcast_in_dim.91
  243.4 4.6 all-to-all-start.4
  248.1 27.1 %all-to-all-done.4 = f32[8,1024,64]{1,2,0:T(8,128)S(1)} async-done(((f32[8,1024,64]{1,2,0:T(8,128)}), f32[8,1024,64]{1,2,0:T(8,128)S(1)}, u32[]{:S(2)}, u32[]{:S(2)}) %all-to-all-start.4) | async-done | bytes 2097184 | tf_op jit(solution)/shard_map/all_to_all | solution.py:22
  276.2 5.3 all-to-all-start.5
  281.6 11.2 %all-to-all-done.5 = bf16[16,64,256]{2,1,0:T(8,128)(2,1)} async-done(((bf16[16,64,256]{2,1,0:T(8,128)(2,1)}), bf16[16,64,256]{2,1,0:T(8,128)(2,1)}, u32[]{:S(2)}, u32[]{:S(2)}) %all-to-all-start.5) | async-done | bytes 524320 | tf_op jit(solution)/shard_map/all_to_all | solution.py:22
  292.8 0.9 slice.159
  294.0 11.7 %cholesky.130 = f32[128,128]{1,0:T(8,128)S(1)} custom-call(f32[128,128]{1,0:T(8,128)S(1)} %cholesky.194), custom_call_target="Cholesky" | custom-call | tf_op jit(solution)/shard_map/jit(cholesky)/cholesky | solution.py:156
  305.7 9.8 %custom-call.13 = f32[1,128,128]{1,2,0:T(8,128)S(1)} custom-call(f32[1,128,128]{2,1,0:T(8,128)S(1)} %get-tuple-element.84), custom_call_target="InvertDiagBlocksLowerTriangular" | custom-call | tf_op jit(solution)/shard_map/jit(cholesky)/cholesky | solution.py:156
  316.0 11.7 %cholesky.147 = f32[128,128]{1,0:T(8,128)S(1)} custom-call(f32[128,128]{1,0:T(8,128)S(1)} %convolution_subtract_fusion.5), custom_call_target="Cholesky" | custom-call | tf_op jit(solution)/shard_map/jit(cholesky)/cholesky | solution.py:156
  329.9 4.3 while.6
  330.8 1.3 bitcast_dynamic-update-slice_fusion.4
  332.8 1.3 bitcast_dynamic-update-slice_fusion.4
  334.2 19.7 %custom-call.14 = f32[2,128,128]{1,2,0:T(8,128)S(1)} custom-call(f32[2,128,128]{2,1,0:T(8,128)S(1)} %get-tuple-element.45), custom_call_target="InvertDiagBlocksLowerTriangular" | custom-call | tf_op jit(solution)/shard_map/jit(_solve_triangular)/triangular_solve | solution.py:157
  356.6 1.0 copy.88
  357.6 1.0 copy.87
  359.3 82.4 %all-reduce.8.cloned.1.call-done = (bf16[1,16,64,256]{3,2,1,0:T(8,128)(2,1)}, bf16[1,16,64,256]{3,2,1,0:T(8,128)(2,1)}) async-done(((bf16[1,16,64,256]{3,2,1,0:T(8,128)(2,1)}, bf16[1,16,64,256]{3,2,1,0:T(8,128)(2,1)}), (bf16[1,16,64,256]{3,2,1,0:T(8,128)(2,1)}, bf16[1,16,64,256]{3,2,1,0:T(8,128)(2,1)})) %all-reduce.8.cloned.1.call-update) | async-done | bytes 1048592 | tf_op jit(solution)/shard_map/psum | solution.py:50
  441.7 1.3 maximum_bitcast_fusion.1
  443.1 9.5 %convolution_subtract_fusion.1 = f32[1024,2048]{1,0:T(8,128)S(1)} fusion(f32[1024,2048]{1,0:T(8,128)} %copy-done.4, f32[1024,256]{0,1:T(8,128)S(1)} %get-tuple-element.91, bf16[2048,256]{1,0:T(8,128)(2,1)S(1)} %bitcast.124), kind=kOutput, calls=%fused_computation.8 | convolution fusion | flops 6444548096 | bytes 18874368 | tf_op jit(solution)/shard_map/dot_general | solution.py:54
  452.6 3.4 copy-done.2
  456.0 1.6 fusion.1
  458.6 31.7 %all_to_all.50 = f32[8,1024,64]{1,2,0:T(8,128)S(1)} all-to-all(f32[8,1024,64]{1,2,0:T(8,128)S(1)} %broadcast_in_dim.96), channel_id=1, replica_groups=mesh['row_0'=4,'row_1'=4,'col'=8] {'col'}, dimensions={0} | all-to-all | bytes 4194304 | tf_op jit(solution)/shard_map/all_to_all | solution.py:22
  490.5 0.9 broadcast_in_dim.97
  491.4 4.8 all-to-all-start.7
  496.7 10.6 %all-to-all-done.7 = bf16[16,64,256]{2,1,0:T(8,128)(2,1)} async-done(((bf16[16,64,256]{2,1,0:T(8,128)(2,1)}), bf16[16,64,256]{2,1,0:T(8,128)(2,1)}, u32[]{:S(2)}, u32[]{:S(2)}) %all-to-all-start.7) | async-done | bytes 524320 | tf_op jit(solution)/shard_map/all_to_all | solution.py:22
  507.3 0.9 slice.164
  508.5 11.7 %cholesky.164 = f32[128,128]{1,0:T(8,128)S(1)} custom-call(f32[128,128]{1,0:T(8,128)S(1)} %cholesky.197), custom_call_target="Cholesky" | custom-call | tf_op jit(solution)/shard_map/jit(cholesky)/cholesky | solution.py:156
  520.3 9.8 %custom-call.15 = f32[1,128,128]{1,2,0:T(8,128)S(1)} custom-call(f32[1,128,128]{2,1,0:T(8,128)S(1)} %get-tuple-element.80), custom_call_target="InvertDiagBlocksLowerTriangular" | custom-call | tf_op jit(solution)/shard_map/jit(cholesky)/cholesky | solution.py:156
  530.6 11.7 %cholesky.181 = f32[128,128]{1,0:T(8,128)S(1)} custom-call(f32[128,128]{1,0:T(8,128)S(1)} %convolution_subtract_fusion.4), custom_call_target="Cholesky" | custom-call | tf_op jit(solution)/shard_map/jit(cholesky)/cholesky | solution.py:156
  545.0 4.3 while.7
  545.9 1.4 bitcast_dynamic-update-slice_fusion.5
  547.9 1.4 bitcast_dynamic-update-slice_fusion.5
  549.3 19.7 %custom-call.16 = f32[2,128,128]{1,2,0:T(8,128)S(1)} custom-call(f32[2,128,128]{2,1,0:T(8,128)S(1)} %get-tuple-element.46), custom_call_target="InvertDiagBlocksLowerTriangular" | custom-call | tf_op jit(solution)/shard_map/jit(_solve_triangular)/triangular_solve | solution.py:157
  571.7 1.0 copy.96
  572.7 1.0 copy.95
  573.8 3.5 scatter.6
  577.2 79.6 %all-reduce.6.cloned.1.call-done = (bf16[1,16,64,256]{3,2,1,0:T(8,128)(2,1)}, bf16[1,16,64,256]{3,2,1,0:T(8,128)(2,1)}) async-done(((bf16[1,16,64,256]{3,2,1,0:T(8,128)(2,1)}, bf16[1,16,64,256]{3,2,1,0:T(8,128)(2,1)}), (bf16[1,16,64,256]{3,2,1,0:T(8,128)(2,1)}, bf16[1,16,64,256]{3,2,1,0:T(8,128)(2,1)})) %all-reduce.6.cloned.1.call-update) | async-done | bytes 1048592 | tf_op jit(solution)/shard_map/psum | solution.py:50
  656.8 1.3 maximum_bitcast_fusion.3
  658.2 9.5 %convolution_subtract_fusion = f32[1024,2048]{1,0:T(8,128)S(1)} fusion(f32[1024,2048]{1,0:T(8,128)} %scatter.6, f32[1024,256]{0,1:T(8,128)S(1)} %get-tuple-element.94, bf16[2048,256]{1,0:T(8,128)(2,1)S(1)} %bitcast.125), kind=kOutput, calls=%fused_computation.7 | convolution fusion | flops 6444548096 | bytes 18874368 | tf_op jit(solution)/shard_map/dot_general | solution.py:54
  667.7 3.4 copy-done.3
  671.1 1.6 fusion
  672.7 3.5 scatter.9
  676.2 7.6 %compare_select_fusion = f32[1024,2048]{1,0:T(8,128)} fusion(f32[1024,2048]{1,0:T(8,128)} %scatter.9, s32[2048]{0:T(1024)S(1)} %fusion.41, s32[1024]{0:T(1024)S(1)} %get-tuple-element.95), kind=kLoop, calls=%fused_computation.6 | loop fusion | flops 4194304 | bytes 16789504 | tf_op jit(solution)/shard_map/jit(_where)/select_n | solution.py:192
  (92 shorter events, 18.4 us)
Async XLA Ops:
  6.5 41.7 %copy-start = (bf16[640,1024]{1,0:T(8,128)(2,1)S(1)}, bf16[640,1024]{1,0:T(8,128)(2,1)}, u32[]{:S(2)}) copy-start(bf16[640,1024]{1,0:T(8,128)(2,1)} %param.17) | copy-start | bytes 3932164
  10.1 10.6 %all-to-all-start = ((f32[8,1,64]{2,1,0:T(1,128)}), f32[8,1,64]{2,1,0:T(1,128)S(1)}, u32[]{:S(2)}, u32[]{:S(2)}) async-start(f32[8,1,64]{2,1,0:T(1,128)} %broadcast_in_dim.87), calls=%async_computation | async-start | bytes 8192 | tf_op jit(solution)/shard_map/all_to_all | solution.py:22
  15.5 89.8 %reduce-scatter.2.cloned.1.call-start = ((), (), s32[]{:S(2)}) async-start(), calls=%async_computation.9 | async-start | bytes 9437184 | tf_op jit(solution)/shard_map/reduce_scatter | solution.py:95
  48.2 1.9 copy-start.7
  129.2 31.5 %all-to-all-start.2 = ((bf16[8,128,1024]{1,2,0:T(8,128)(2,1)}), bf16[8,128,1024]{1,2,0:T(8,128)(2,1)}, u32[]{:S(2)}, u32[]{:S(2)}) async-start(bf16[8,128,1024]{1,2,0:T(8,128)(2,1)} %broadcast_in_dim.89), calls=%async_computation.3 | async-start | bytes 4194304 | tf_op jit(solution)/shard_map/all_to_all | solution.py:22
  133.6 96.3 %all-gather.2.cloned.1.call-start = ((), (), s32[]{:S(2)}) async-start(), calls=%async_computation.10 | async-start | bytes 4456448 | tf_op jit(solution)/shard_map/all_gather | solution.py:112
  238.1 3.4 copy-start.4
  243.4 31.8 %all-to-all-start.4 = ((f32[8,1024,64]{1,2,0:T(8,128)}), f32[8,1024,64]{1,2,0:T(8,128)S(1)}, u32[]{:S(2)}, u32[]{:S(2)}) async-start(f32[8,1024,64]{1,2,0:T(8,128)} %broadcast_in_dim.91), calls=%async_computation.5 | async-start | bytes 4194304 | tf_op jit(solution)/shard_map/all_to_all | solution.py:22
  276.2 16.7 %all-to-all-start.5 = ((bf16[16,64,256]{2,1,0:T(8,128)(2,1)}), bf16[16,64,256]{2,1,0:T(8,128)(2,1)}, u32[]{:S(2)}, u32[]{:S(2)}) async-start(bf16[16,64,256]{2,1,0:T(8,128)(2,1)} %broadcast_in_dim.92), calls=%async_computation.6 | async-start | bytes 1048576 | tf_op jit(solution)/shard_map/all_to_all | solution.py:22
  281.5 160.2 %all-reduce.8.cloned.1.call-start = ((), (), s32[]{:S(2)}) async-start(), calls=%async_computation.12 | async-start | bytes 2097152 | tf_op jit(solution)/shard_map/psum | solution.py:50
  452.6 3.4 copy-start.2
  457.6 0.8 copy-start.5
  491.4 16.0 %all-to-all-start.7 = ((bf16[16,64,256]{2,1,0:T(8,128)(2,1)}), bf16[16,64,256]{2,1,0:T(8,128)(2,1)}, u32[]{:S(2)}, u32[]{:S(2)}) async-start(bf16[16,64,256]{2,1,0:T(8,128)(2,1)} %broadcast_in_dim.97), calls=%async_computation.8 | async-start | bytes 1048576 | tf_op jit(solution)/shard_map/all_to_all | solution.py:22
  496.2 160.7 %all-reduce.6.cloned.1.call-start = ((), (), s32[]{:S(2)}) async-start(), calls=%async_computation.11 | async-start | bytes 2097152 | tf_op jit(solution)/shard_map/psum | solution.py:50
  570.2 3.6 copy-start.6
  667.7 3.4 copy-start.3
  676.2 7.6 %copy-start.1 = (bf16[640,1024]{1,0:T(8,128)(2,1)S(1)}, bf16[640,1024]{1,0:T(8,128)(2,1)}, u32[]{:S(2)}) copy-start(bf16[640,1024]{1,0:T(8,128)(2,1)} %param.17) | copy-start | bytes 3932164
Sparse Core Ops, SparseCore 0:
  56.4 48.8 reduce-scatter.1
  167.8 62.0 all-gather.1
  358.8 82.9 all-reduce.7
  573.9 82.8 all-reduce.5
where the time goes:
time: 700 us; the launch traced here: 690 us
  waiting for transfers between devices  316 us (45%)
  other arithmetic  129 us (18%)
  blocking collectives  115 us (16%)
  local copies, waits for them, and re-layouts  48.1 us (7%)
  matrix products  40.5 us (6%)
  starting transfers between devices  25 us (4%)
  between operations  16.4 us (2%)
    psum x2, waiting for transfers between devices, broadcast(): return lax.psum(kept, axis)  162 us
    all_to_all x5, waiting for transfers between devices, copy_for_each(): return lax.all_to_all(copies, axis, split_axis=0, concat_axis=0, tiled=True)  81.3 us
    another operation x13, other arithmetic, on_device(): lower_factor = jnp.linalg.cholesky(diag_rows[row_offset:row_offset + PANEL])  68.7 us
    all_to_all x2, blocking collectives, copy_for_each(): return lax.all_to_all(copies, axis, split_axis=0, concat_axis=0, tiled=True)  58.3 us
    reduce_scatter x1, waiting for transfers between devices, on_device(): lax.psum_scatter(jnp.concatenate([gate_block, up_block], axis=1), 'col',...  49.1 us
    another operation x5, other arithmetic, on_device(): jax.scipy.linalg.solve_triangular(lower_factor, panel_rows.T, lower=True)  39.4 us
    all_to_all x1, blocking collectives, on_device(): lax.all_to_all(grouped, ROW, split_axis=1, concat_axis=1, tiled=True)  35.8 us
    all_to_all x5, starting transfers between devices, copy_for_each(): return lax.all_to_all(copies, axis, split_axis=0, concat_axis=0, tiled=True)  24.4 us
  transfers between devices with their start and end apart: 9, of which 9 were waited for; matrix products, arithmetic and copies ran while one was open for 1% of the time, Pallas kernels for 0%

commit v1 on v0

--- a/solution.py
+++ b/solution.py
@@ -11,6 +11,18 @@
 ROW = ("row_0", "row_1")
 EPSILON = 1e-06
 HIGHEST_PRECISION = lax.Precision.HIGHEST
+
+
+def _expand_rails(raw, on_dim):
+    return jnp.concatenate(
+        lax.all_to_all(
+            jnp.stack([raw for _ in range(lax.axis_size(ROW))]),
+            axis_name=ROW,
+            split_axis=0,
+            concat_axis=0,
+        ),
+        axis=on_dim,
+    )
 
 
 def by_axis(array, axes):
@@ -109,7 +121,7 @@
     col_pick = lax.dynamic_index_in_dim(col_split, col_rank, axis=2, keepdims=False).reshape(
         prompts, tiles_here // col_devices * TILE
     )
-    col_keys = lax.all_gather(col_pick, ROW, axis=1, tiled=True)
+    col_keys = _expand_rails(col_pick, 1)
     keys_outer = lax.dot_general(
         row_keys, col_keys, (((0,), (0,)), ((), ())), preferred_element_type=jnp.float32
     )

time: 700 us -> 716 us (1.023)
  blocking collectives: 115 us -> 161 us
  waiting for transfers between devices: 316 us -> 292 us
    all_to_all x2 -> x3, blocking collectives: 58.3 us -> 88.2 us  [copy_for_each(): return lax.all_to_all(copies, axis, split_axis=0, concat_axis=0, tiled=True)]
    all_to_all x0 -> x1, waiting for transfers between devices: none -> 26.9 us  [on_device(): lax.all_to_all(grouped, ROW, split_axis=1, concat_axis=1, tiled=True)]
    all_to_all x5 -> x4, waiting for transfers between devices: 81.3 us -> 54.4 us  [copy_for_each(): return lax.all_to_all(copies, axis, split_axis=0, concat_axis=0, tiled=True)]
    all_gather x1 -> x0, waiting for transfers between devices: 24.1 us -> none  [on_device(): col_keys = lax.all_gather(col_pick, ROW, axis=1, tiled=True)]
    all_to_all x1, blocking collectives: 35.8 us -> 52.3 us  [_expand_rails(): lax.all_to_all(jnp.stack([raw for _ in range(lax.axis_size(ROW))]), axis_...]
    all_to_all x5 -> x4, starting transfers between devices: 24.4 us -> 18.4 us  [copy_for_each(): return lax.all_to_all(copies, axis, split_axis=0, concat_axis=0, tiled=True)]
  transfers between devices with their start and end apart: 9 -> 8, of which waited for: 9 -> 8; matrix products, arithmetic and copies ran while one was open for 1% -> 1% of each run, Pallas kernels for 0% -> 0%
where the time goes in v1:
time: 716 us; the launch traced here: 708 us
  waiting for transfers between devices  292 us (41%)
  blocking collectives  161 us (22%)
  other arithmetic  129 us (18%)
  local copies, waits for them, and re-layouts  45.1 us (6%)
  matrix products  40 us (6%)
  starting transfers between devices  23.3 us (3%)
  between operations  16.4 us (2%)
    psum x2, waiting for transfers between devices, broadcast(): return lax.psum(kept, axis)  162 us
    all_to_all x3, blocking collectives, copy_for_each(): return lax.all_to_all(copies, axis, split_axis=0, concat_axis=0, tiled=True)  88.2 us
    another operation x13, other arithmetic, on_device(): lower_factor = jnp.linalg.cholesky(diag_rows[row_offset:row_offset + PANEL])  68.7 us
    all_to_all x4, waiting for transfers between devices, copy_for_each(): return lax.all_to_all(copies, axis, split_axis=0, concat_axis=0, tiled=True)  54.4 us
    all_to_all x1, blocking collectives, _expand_rails(): lax.all_to_all(jnp.stack([raw for _ in range(lax.axis_size(ROW))]), axis_...  52.3 us
    reduce_scatter x1, waiting for transfers between devices, on_device(): lax.psum_scatter(jnp.concatenate([gate_block, up_block], axis=1), 'col',...  49.1 us
    another operation x5, other arithmetic, on_device(): jax.scipy.linalg.solve_triangular(lower_factor, panel_rows.T, lower=True)  39.4 us
    all_to_all x1, waiting for transfers between devices, on_device(): lax.all_to_all(grouped, ROW, split_axis=1, concat_axis=1, tiled=True)  26.9 us
  transfers between devices with their start and end apart: 8, of which 8 were waited for; matrix products, arithmetic and copies ran while one was open for 1% of the time, Pallas kernels for 0%

profile of v1, /device:TPU:0, one launch (start us, length us, event | category | flops | bytes accessed | tf_op | source)
XLA Modules:
  0.0 707.6 jit_solution(16466762456083549275)
XLA Ops:
  7.4 2.0 convert_reduce_fusion
  10.1 5.4 all-to-all-start
  15.6 5.1 all-to-all-done
  21.7 26.6 %all_to_all.53 = bf16[16,64,640]{2,1,0:T(8,128)(2,1)S(1)} all-to-all(bf16[16,64,640]{2,1,0:T(8,128)(2,1)S(1)} %broadcast_in_dim.88), channel_id=1, replica_groups=mesh['row_0'=4,'row_1'=4,'col'=8] {'row_0','row_1'}, dimensions={0} | all-to-all | bytes 2621440 | tf_op jit(solution)/shard_map/all_to_all | solution.py:34
  48.2 1.9 fusion.61
  50.1 1.9 fusion.60
  52.0 4.2 pad_maximum_fusion
  56.2 49.1 %reduce-scatter.2.cloned.1.call-done = f32[128,2048]{0,1:T(8,128)} async-done(((f32[1024,2048]{0,1:T(8,128)}), f32[128,2048]{0,1:T(8,128)}) %reduce-scatter.2.cloned.1.call-update) | async-done | bytes 1048592 | tf_op jit(solution)/shard_map/reduce_scatter | solution.py:107
  105.3 1.4 multiply_reduce_fusion
  106.7 10.4 %psum.42 = f32[128]{0:T(128)S(1)} all-reduce(f32[128]{0:T(128)S(1)} %get-tuple-element.67), channel_id=1, replica_groups=mesh['row_0'=4,'row_1'=4,'col'=8] {'row_0'}, use_global_device_ids=true, to_apply=%region_5.6 | all-reduce | flops 128 | bytes 1024 | tf_op jit(solution)/shard_map/psum | solution.py:29
  117.1 10.5 %psum.43 = f32[128]{0:T(128)S(1)} all-reduce(f32[128]{0:T(128)S(1)} %psum.42), channel_id=1, replica_groups=mesh['row_0'=4,'row_1'=4,'col'=8] {'row_1'}, use_global_device_ids=true, to_apply=%region_6.7 | all-reduce | flops 128 | bytes 1024 | tf_op jit(solution)/shard_map/psum | solution.py:29
  127.9 30.0 %all_to_all.54 = bf16[8,128,1024]{1,2,0:T(8,128)(2,1)S(1)} all-to-all(bf16[8,128,1024]{1,2,0:T(8,128)(2,1)S(1)} %broadcast_in_dim.89), channel_id=1, replica_groups=mesh['row_0'=4,'row_1'=4,'col'=8] {'col'}, dimensions={0} | all-to-all | bytes 4194304 | tf_op jit(solution)/shard_map/all_to_all | solution.py:34
  157.8 1.4 copy.81
  159.2 2.3 all_to_all.36
  161.5 4.4 all-to-all-start.3
  165.9 2.3 reshape_reshape.3
  168.3 1.0 constant_dynamic-slice_fusion.2
  169.2 26.9 %all-to-all-done.3 = bf16[1024,16,64]{0,2,1:T(8,128)(2,1)} async-done(((bf16[1024,16,64]{0,2,1:T(8,128)(2,1)}), bf16[1024,16,64]{0,2,1:T(8,128)(2,1)}, u32[]{:S(2)}, u32[]{:S(2)}) %all-to-all-start.3) | async-done | bytes 2097184 | tf_op jit(solution)/shard_map/all_to_all | solution.py:119
  196.6 52.3 %all_to_all.55 = bf16[16,1024,128]{1,2,0:T(8,128)(2,1)S(1)} all-to-all(bf16[16,1024,128]{1,2,0:T(8,128)(2,1)S(1)} %stack.21), channel_id=1, replica_groups=mesh['row_0'=4,'row_1'=4,'col'=8] {'row_0','row_1'}, dimensions={0} | all-to-all | bytes 8388608 | tf_op jit(solution)/shard_map/all_to_all | solution.py:18
  248.9 7.8 %multiply_add_fusion = f32[1024,2048]{1,0:T(8,128)S(1)} fusion(f32[1024,2048]{1,0:T(8,128)} %param.18, bf16[1024,1024]{0,1:T(8,128)(2,1)} %bitcast.2, bf16[1024,2048]{0,1:T(8,128)(2,1)S(1)} %bitcast.129), kind=kOutput, calls=%fused_computation.5 | convolution fusion | flops 4299161600 | bytes 23068672 | tf_op jit(solution)/shard_map/dot_general | solution.py:125
  256.7 3.4 copy-done.4
  260.3 1.6 broadcast_in_dim.91
  262.0 4.0 all-to-all-start.5
  265.9 27.2 %all-to-all-done.5 = f32[8,1024,64]{1,2,0:T(8,128)S(1)} async-done(((f32[8,1024,64]{1,2,0:T(8,128)}), f32[8,1024,64]{1,2,0:T(8,128)S(1)}, u32[]{:S(2)}, u32[]{:S(2)}) %all-to-all-start.5) | async-done | bytes 2097184 | tf_op jit(solution)/shard_map/all_to_all | solution.py:34
  293.2 0.9 broadcast_in_dim.92
  294.1 4.2 all-to-all-start.6
  298.5 11.4 %all-to-all-done.6 = bf16[16,64,256]{2,1,0:T(8,128)(2,1)} async-done(((bf16[16,64,256]{2,1,0:T(8,128)(2,1)}), bf16[16,64,256]{2,1,0:T(8,128)(2,1)}, u32[]{:S(2)}, u32[]{:S(2)}) %all-to-all-start.6) | async-done | bytes 524320 | tf_op jit(solution)/shard_map/all_to_all | solution.py:34
  309.9 0.9 slice.159
  311.1 11.7 %cholesky.130 = f32[128,128]{1,0:T(8,128)S(1)} custom-call(f32[128,128]{1,0:T(8,128)S(1)} %cholesky.194), custom_call_target="Cholesky" | custom-call | tf_op jit(solution)/shard_map/jit(cholesky)/cholesky | solution.py:168
  322.8 9.8 %custom-call.13 = f32[1,128,128]{1,2,0:T(8,128)S(1)} custom-call(f32[1,128,128]{2,1,0:T(8,128)S(1)} %get-tuple-element.84), custom_call_target="InvertDiagBlocksLowerTriangular" | custom-call | tf_op jit(solution)/shard_map/jit(cholesky)/cholesky | solution.py:168
  333.1 11.7 %cholesky.147 = f32[128,128]{1,0:T(8,128)S(1)} custom-call(f32[128,128]{1,0:T(8,128)S(1)} %convolution_subtract_fusion.5), custom_call_target="Cholesky" | custom-call | tf_op jit(solution)/shard_map/jit(cholesky)/cholesky | solution.py:168
  347.0 4.3 while.6
  347.9 1.3 bitcast_dynamic-update-slice_fusion.4
  349.9 1.3 bitcast_dynamic-update-slice_fusion.4
  351.3 19.7 %custom-call.14 = f32[2,128,128]{1,2,0:T(8,128)S(1)} custom-call(f32[2,128,128]{2,1,0:T(8,128)S(1)} %get-tuple-element.45), custom_call_target="InvertDiagBlocksLowerTriangular" | custom-call | tf_op jit(solution)/shard_map/jit(_solve_triangular)/triangular_solve | solution.py:169
  373.7 1.0 copy.88
  374.7 1.0 copy.87
  376.4 82.4 %all-reduce.8.cloned.1.call-done = (bf16[1,16,64,256]{3,2,1,0:T(8,128)(2,1)}, bf16[1,16,64,256]{3,2,1,0:T(8,128)(2,1)}) async-done(((bf16[1,16,64,256]{3,2,1,0:T(8,128)(2,1)}, bf16[1,16,64,256]{3,2,1,0:T(8,128)(2,1)}), (bf16[1,16,64,256]{3,2,1,0:T(8,128)(2,1)}, bf16[1,16,64,256]{3,2,1,0:T(8,128)(2,1)})) %all-reduce.8.cloned.1.call-update) | async-done | bytes 1048592 | tf_op jit(solution)/shard_map/psum | solution.py:62
  458.8 1.3 maximum_bitcast_fusion.1
  460.2 9.5 %convolution_subtract_fusion.1 = f32[1024,2048]{1,0:T(8,128)S(1)} fusion(f32[1024,2048]{1,0:T(8,128)} %copy-done.4, f32[1024,256]{0,1:T(8,128)S(1)} %get-tuple-element.91, bf16[2048,256]{1,0:T(8,128)(2,1)S(1)} %bitcast.127), kind=kOutput, calls=%fused_computation.8 | convolution fusion | flops 6444548096 | bytes 18874368 | tf_op jit(solution)/shard_map/dot_general | solution.py:66
  469.7 3.4 copy-done.2
  473.1 1.6 fusion.1
  475.8 31.7 %all_to_all.56 = f32[8,1024,64]{1,2,0:T(8,128)S(1)} all-to-all(f32[8,1024,64]{1,2,0:T(8,128)S(1)} %broadcast_in_dim.96), channel_id=1, replica_groups=mesh['row_0'=4,'row_1'=4,'col'=8] {'col'}, dimensions={0} | all-to-all | bytes 4194304 | tf_op jit(solution)/shard_map/all_to_all | solution.py:34
  507.6 0.9 broadcast_in_dim.97
  508.5 4.8 all-to-all-start.8
  513.8 10.6 %all-to-all-done.8 = bf16[16,64,256]{2,1,0:T(8,128)(2,1)} async-done(((bf16[16,64,256]{2,1,0:T(8,128)(2,1)}), bf16[16,64,256]{2,1,0:T(8,128)(2,1)}, u32[]{:S(2)}, u32[]{:S(2)}) %all-to-all-start.8) | async-done | bytes 524320 | tf_op jit(solution)/shard_map/all_to_all | solution.py:34
  524.5 0.9 slice.164
  525.6 11.7 %cholesky.164 = f32[128,128]{1,0:T(8,128)S(1)} custom-call(f32[128,128]{1,0:T(8,128)S(1)} %cholesky.197), custom_call_target="Cholesky" | custom-call | tf_op jit(solution)/shard_map/jit(cholesky)/cholesky | solution.py:168
  537.4 9.8 %custom-call.15 = f32[1,128,128]{1,2,0:T(8,128)S(1)} custom-call(f32[1,128,128]{2,1,0:T(8,128)S(1)} %get-tuple-element.80), custom_call_target="InvertDiagBlocksLowerTriangular" | custom-call | tf_op jit(solution)/shard_map/jit(cholesky)/cholesky | solution.py:168
  547.7 11.7 %cholesky.181 = f32[128,128]{1,0:T(8,128)S(1)} custom-call(f32[128,128]{1,0:T(8,128)S(1)} %convolution_subtract_fusion.4), custom_call_target="Cholesky" | custom-call | tf_op jit(solution)/shard_map/jit(cholesky)/cholesky | solution.py:168
  562.1 4.3 while.7
  563.0 1.4 bitcast_dynamic-update-slice_fusion.5
  565.0 1.4 bitcast_dynamic-update-slice_fusion.5
  566.4 19.7 %custom-call.16 = f32[2,128,128]{1,2,0:T(8,128)S(1)} custom-call(f32[2,128,128]{2,1,0:T(8,128)S(1)} %get-tuple-element.46), custom_call_target="InvertDiagBlocksLowerTriangular" | custom-call | tf_op jit(solution)/shard_map/jit(_solve_triangular)/triangular_solve | solution.py:169
  588.8 1.0 copy.96
  589.8 1.0 copy.95
  590.9 3.5 scatter.6
  594.4 79.6 %all-reduce.6.cloned.1.call-done = (bf16[1,16,64,256]{3,2,1,0:T(8,128)(2,1)}, bf16[1,16,64,256]{3,2,1,0:T(8,128)(2,1)}) async-done(((bf16[1,16,64,256]{3,2,1,0:T(8,128)(2,1)}, bf16[1,16,64,256]{3,2,1,0:T(8,128)(2,1)}), (bf16[1,16,64,256]{3,2,1,0:T(8,128)(2,1)}, bf16[1,16,64,256]{3,2,1,0:T(8,128)(2,1)})) %all-reduce.6.cloned.1.call-update) | async-done | bytes 1048592 | tf_op jit(solution)/shard_map/psum | solution.py:62
  673.9 1.3 maximum_bitcast_fusion.3
  675.3 9.5 %convolution_subtract_fusion = f32[1024,2048]{1,0:T(8,128)S(1)} fusion(f32[1024,2048]{1,0:T(8,128)} %scatter.6, f32[1024,256]{0,1:T(8,128)S(1)} %get-tuple-element.94, bf16[2048,256]{1,0:T(8,128)(2,1)S(1)} %bitcast.128), kind=kOutput, calls=%fused_computation.7 | convolution fusion | flops 6444548096 | bytes 18874368 | tf_op jit(solution)/shard_map/dot_general | solution.py:66
  684.8 3.4 copy-done.3
  688.2 1.6 fusion
  689.8 3.5 scatter.9
  693.3 7.6 %compare_select_fusion = f32[1024,2048]{1,0:T(8,128)} fusion(f32[1024,2048]{1,0:T(8,128)} %scatter.9, s32[2048]{0:T(1024)S(1)} %fusion.41, s32[1024]{0:T(1024)S(1)} %get-tuple-element.95), kind=kLoop, calls=%fused_computation.6 | loop fusion | flops 4194304 | bytes 16789504 | tf_op jit(solution)/shard_map/jit(_where)/select_n | solution.py:204
  (91 shorter events, 18.2 us)
Async XLA Ops:
  6.5 41.7 %copy-start = (bf16[640,1024]{1,0:T(8,128)(2,1)S(1)}, bf16[640,1024]{1,0:T(8,128)(2,1)}, u32[]{:S(2)}) copy-start(bf16[640,1024]{1,0:T(8,128)(2,1)} %param.17) | copy-start | bytes 3932164
  10.1 10.6 %all-to-all-start = ((f32[8,1,64]{2,1,0:T(1,128)}), f32[8,1,64]{2,1,0:T(1,128)S(1)}, u32[]{:S(2)}, u32[]{:S(2)}) async-start(f32[8,1,64]{2,1,0:T(1,128)} %broadcast_in_dim.87), calls=%async_computation | async-start | bytes 8192 | tf_op jit(solution)/shard_map/all_to_all | solution.py:34
  15.5 89.8 %reduce-scatter.2.cloned.1.call-start = ((), (), s32[]{:S(2)}) async-start(), calls=%async_computation.10 | async-start | bytes 9437184 | tf_op jit(solution)/shard_map/reduce_scatter | solution.py:107
  48.2 1.9 copy-start.7
  161.5 34.6 %all-to-all-start.3 = ((bf16[1024,16,64]{0,2,1:T(8,128)(2,1)}), bf16[1024,16,64]{0,2,1:T(8,128)(2,1)}, u32[]{:S(2)}, u32[]{:S(2)}) async-start(bf16[1024,16,64]{0,2,1:T(8,128)(2,1)} %all_to_all.36), calls=%async_computation.4 | async-start | bytes 4194304 | tf_op jit(solution)/shard_map/all_to_all | solution.py:119
  256.7 3.4 copy-start.4
  262.0 31.2 %all-to-all-start.5 = ((f32[8,1024,64]{1,2,0:T(8,128)}), f32[8,1024,64]{1,2,0:T(8,128)S(1)}, u32[]{:S(2)}, u32[]{:S(2)}) async-start(f32[8,1024,64]{1,2,0:T(8,128)} %broadcast_in_dim.91), calls=%async_computation.6 | async-start | bytes 4194304 | tf_op jit(solution)/shard_map/all_to_all | solution.py:34
  294.1 15.8 %all-to-all-start.6 = ((bf16[16,64,256]{2,1,0:T(8,128)(2,1)}), bf16[16,64,256]{2,1,0:T(8,128)(2,1)}, u32[]{:S(2)}, u32[]{:S(2)}) async-start(bf16[16,64,256]{2,1,0:T(8,128)(2,1)} %broadcast_in_dim.92), calls=%async_computation.7 | async-start | bytes 1048576 | tf_op jit(solution)/shard_map/all_to_all | solution.py:34
  298.3 160.5 %all-reduce.8.cloned.1.call-start = ((), (), s32[]{:S(2)}) async-start(), calls=%async_computation.12 | async-start | bytes 2097152 | tf_op jit(solution)/shard_map/psum | solution.py:62
  469.7 3.4 copy-start.2
  474.7 0.8 copy-start.5
  508.5 16.0 %all-to-all-start.8 = ((bf16[16,64,256]{2,1,0:T(8,128)(2,1)}), bf16[16,64,256]{2,1,0:T(8,128)(2,1)}, u32[]{:S(2)}, u32[]{:S(2)}) async-start(bf16[16,64,256]{2,1,0:T(8,128)(2,1)} %broadcast_in_dim.97), calls=%async_computation.9 | async-start | bytes 1048576 | tf_op jit(solution)/shard_map/all_to_all | solution.py:34
  513.3 160.7 %all-reduce.6.cloned.1.call-start = ((), (), s32[]{:S(2)}) async-start(), calls=%async_computation.11 | async-start | bytes 2097152 | tf_op jit(solution)/shard_map/psum | solution.py:62
  587.3 3.6 copy-start.6
  684.8 3.4 copy-start.3
  693.3 7.6 %copy-start.1 = (bf16[640,1024]{1,0:T(8,128)(2,1)S(1)}, bf16[640,1024]{1,0:T(8,128)(2,1)}, u32[]{:S(2)}) copy-start(bf16[640,1024]{1,0:T(8,128)(2,1)} %param.17) | copy-start | bytes 3932164
Sparse Core Ops, SparseCore 0:
  56.4 48.8 reduce-scatter.1
  375.9 82.9 all-reduce.7
  591.0 82.8 all-reduce.5
